TPU v7x, 32 devices: a whole 2x2x4 slice. The times are simulated.
32 devices in a mesh: gx: 4 (over x, core), gy: 2 (over y), gz: 4 (over z).
Axes of the slice: x: 2, y: 2, z: 4, core: 2. Of those that a mesh axis runs over, the one named last changes fastest.
Arguments:
- initial: float32 [12, 32, 16, 512], P(None, 'gx', 'gy', 'gz'), may hold values from -4 to 4
- source: float32 [12, 32, 16, 512], P(None, 'gx', 'gy', 'gz'), may hold values from -6 to 6
- classes: int32 [32, 16, 512], P('gx', 'gy', 'gz'), may hold values from 0 to 15
- coupling: float32 [16], replicated, may hold values from 0.3 to 3
- owner: int32 [32, 16, 512], P('gx', 'gy', 'gz'), may hold values from 0 to 4095
- model: float32 [8, 8, 512], P('gx', 'gy', 'gz'), may hold values from -4 to 4
Outputs:
- fields: float32 [12, 32, 16, 512], P(None, 'gx', 'gy', 'gz')
- gradient: float32 [8, 8, 512], P('gx', 'gy', 'gz')
Inputs may be any that keep to these rules, and one draw needn't show every extreme that they name: owner v of a cell at (x, y, z) names inversion cell v mod (1024) of the block of inversion cells with x index x // 8, y index y // 8 and depth index v // 1024.
All inputs are finite; a program needn't handle non-finite values.
Results may differ from a plain program's by a relative error of at most 0.00002.
Values sent between devices are 32-bit elements; how exact they have to be, the bound alone decides.
A program may use at most 64 MiB of HBM per device.

v0:
```python
import functools

import jax
import jax.numpy as jnp
from jax import lax
from jax.experimental import pallas as pl
from jax.experimental.pallas import tpu as pltpu
from jax.sharding import PartitionSpec as P

SWEEPS = 4
MESH = pl.DeviceIdType.MESH
AXES = ("gx", "gy", "gz")
F32 = jnp.float32
BF16 = jnp.bfloat16


def kernel(
    sizes, init_hbm, src_hbm, cls_hbm, coup, own_hbm, mod_hbm, out, grad,
    init, src, cls, own, mod, f, part_next, const, ab, hx, hy, hz, sy, sz, hm, lo_hot, hi_hot, part, rs,
    load_sem, send_sem, recv_sem, msend, mrecv, rsend, rrecv,
):
    chans, nx, ny, nz = init.shape
    pairs = chans // 2
    per_vreg = chans * nx // 2
    pos = [lax.axis_index(a) for a in AXES]
    has = [(pos[i] > 0, pos[i] < sizes[i] - 1) for i in range(3)]
    n = sizes[2]
    peers = [lax.rem(pos[2] + d, n) for d in range(1, n)]
    ends = [[pos[i] - 1, pos[i] + 1] for i in range(3)]

    barrier = pltpu.get_barrier_semaphore()
    for i in range(2):
        for side in range(2):

            @pl.when(has[i][side])
            def _():
                pl.semaphore_signal(
                    barrier, inc=1, device_id={AXES[i]: ends[i][side]}, device_id_type=MESH
                )

    for d in range(1, n):
        pl.semaphore_signal(barrier, inc=1, device_id={"gz": peers[d - 1]}, device_id_type=MESH)
    greeted = n - 1
    for i in range(2):
        for side in range(2):
            greeted = greeted + has[i][side].astype(jnp.int32)

    loads = [
        pltpu.make_async_copy(a, b, load_sem.at[k])
        for k, (a, b) in enumerate(
            (
                (init_hbm, init), (mod_hbm, mod), (cls_hbm, cls), (src_hbm, src), (own_hbm, own),
            )
        )
    ]
    for load in loads:
        load.start()

    lane = lax.broadcasted_iota(jnp.int32, (ny, nz), 1)
    sub = lax.broadcasted_iota(jnp.int32, (ny, nz), 0)
    lane3 = lax.broadcasted_iota(jnp.int32, (nx, ny, nz), 2)
    sub3 = lax.broadcasted_iota(jnp.int32, (nx, ny, nz), 1)

    for i, halo in enumerate((hx, hy, hz)):
        for side in range(2):

            @pl.when(jnp.logical_not(has[i][side]))
            def _():
                halo[:, side] = jnp.zeros((SWEEPS,) + halo.shape[2:], F32)
                hm[2 * i + side] = jnp.zeros(hm.shape[1:], F32)

    def face(s, i, side):
        cells = init if s == 0 else f.at[s - 1]
        if i == 0:
            source = cells.at[:, 0 if side == 0 else nx - 1]
            halo = hx
        elif i == 1:
            source = sy.at[s, side]
            halo = hy
        else:
            source = sz.at[s]
            halo = hz
        return pltpu.make_async_remote_copy(
            src_ref=source,
            dst_ref=halo.at[s, 1 - side],
            send_sem=send_sem.at[s, 2 * i + side],
            recv_sem=recv_sem.at[s, 2 * i + 1 - side],
            device_id={AXES[i]: ends[i][side]},
            device_id_type=MESH,
        )

    def model_copy(i, side):
        return pltpu.make_async_remote_copy(
            src_ref=mod,
            dst_ref=hm.at[2 * i + 1 - side],
            send_sem=msend.at[2 * i + side],
            recv_sem=mrecv.at[2 * i + 1 - side],
            device_id={AXES[i]: ends[i][side]},
            device_id_type=MESH,
        )

    def start(make, i):
        for side in range(2):

            @pl.when(has[i][side])
            def _():
                make(i, side).start()

    def wait_recv(make, i):
        for side in range(2):

            @pl.when(has[i][side])
            def _():
                make(i, 1 - side).wait_recv()

    def wait_send(make, i):
        for side in range(2):

            @pl.when(has[i][side])
            def _():
                make(i, side).wait_send()

    def pack_y(cells, s):
        flat = cells.reshape(chans * nx * ny, nz)
        for c in range(chans):
            for side, row in ((0, 0), (1, ny - 1)):
                sy[s, side, c] = flat[pl.ds(c * nx * ny + row, nx, stride=ny), :]

    def pack_z(acc, value, j):
        return jnp.where((lane >> 1) == j, pltpu.roll(value, 2 * j + 1, 1), acc)

    loads[0].wait()
    pack_y(init, 0)
    for g in range(2):
        acc = jnp.zeros((ny, nz), F32)
        for j in range(per_vreg):
            c, x = divmod(g * per_vreg + j, nx)
            acc = pack_z(acc, init[c, x], j)
        sz[0, g] = acc

    pl.semaphore_wait(barrier, greeted)
    for i in range(3):
        start(functools.partial(face, 0), i)
    loads[1].wait()
    for i in range(3):
        start(model_copy, i)

    loads[2].wait()
    classes = cls[...]
    kappa = jnp.zeros(classes.shape, F32)
    for k in range(coup.shape[0]):
        kappa = jnp.where(classes == k, coup[k], kappa)
    scale = 0.8 / (36.0 + kappa * kappa)
    ab[0] = 6.0 * scale
    ab[1] = kappa * scale
    ab[2] = kappa

    def shifted(v):
        zero = jnp.zeros((1, ny, nz), F32)
        total = jnp.concatenate([zero, v[:-1]], 0) + jnp.concatenate([v[1:], zero], 0)
        total = total + jnp.where(sub3 == 0, 0.0, pltpu.roll(v, 1, 1))
        total = total + jnp.where(sub3 == ny - 1, 0.0, pltpu.roll(v, ny - 1, 1))
        total = total + jnp.where(lane3 == 0, 0.0, pltpu.roll(v, 1, 2))
        return total + jnp.where(lane3 == nz - 1, 0.0, pltpu.roll(v, nz - 1, 2))

    def local(s):
        cells = init if s == 0 else f.at[s - 1]

        def one(p, carry):
            a, b = ab[0], ab[1]
            fr, fi = cells[2 * p], cells[2 * p + 1]
            if s == 0:
                sr, si = src[2 * p], src[2 * p + 1]
                cr, ci = a * sr + b * si, a * si - b * sr
                const[2 * p] = cr
                const[2 * p + 1] = ci
            else:
                cr, ci = const[2 * p], const[2 * p + 1]
            tr, ti = shifted(fr), shifted(fi)
            part_next[2 * p] = cr + 0.2 * fr + (a * tr + b * ti)
            part_next[2 * p + 1] = ci + 0.2 * fi + (a * ti - b * tr)
            return carry

        lax.fori_loop(0, pairs, one, 0, unroll=True)

    def finish(s, planes, accs):
        results = []
        cells = out if s == SWEEPS - 1 else f.at[s]
        last = s == SWEEPS - 1
        merged = [
            jnp.where((lane & 1) == 0, hz[s, 0, g], pltpu.roll(hz[s, 1, g], nz - 2, 1))
            for g in range(2)
        ]
        edge = (lane == 0) | (lane == nz - 1)

        for g in range(2):

            def one(q, acc):
                for x in planes:
                    sums = []
                    for r in range(2):
                        c = g * (chans // 2) + 2 * q + r
                        j = (2 * q + r) * nx + x
                        low = jnp.broadcast_to(hy[s, 0, c, x : x + 1, :], (ny, nz))
                        high = jnp.broadcast_to(hy[s, 1, c, x : x + 1, :], (ny, nz))
                        h = jnp.where(sub == 0, low, jnp.where(sub == ny - 1, high, 0.0))
                        h = h + jnp.where(edge, pltpu.roll(merged[g], nz - 2 * j, 1), 0.0)
                        if x == 0:
                            h = h + hx[s, 0, c]
                        if x == nx - 1:
                            h = h + hx[s, 1, c]
                        sums.append(h)
                    a, b = ab[0, x], ab[1, x]
                    c = g * (chans // 2) + 2 * q
                    nr = part_next[c, x] + (a * sums[0] + b * sums[1])
                    ni = part_next[c + 1, x] + (a * sums[1] - b * sums[0])
                    cells[c, x] = nr
                    cells[c + 1, x] = ni
                    if not last:
                        acc = pack_z(acc, nr, 2 * q * nx + x)
                        acc = pack_z(acc, ni, (2 * q + 1) * nx + x)
                return acc

            first = jnp.zeros((ny, nz), F32) if accs is None else accs[g]
            results.append(lax.fori_loop(0, pairs // 2, one, first, unroll=True))
        return results

    groups = hi_hot.shape[0]

    def hots(x0, x1):
        rows = lax.broadcasted_iota(jnp.int32, (16, nz), 0)
        bands = [(rows + 16 * k).astype(F32).astype(BF16) for k in range(max(nz, groups) // 16)]
        yes, no = jnp.ones((16, nz), BF16), jnp.zeros((16, nz), BF16)

        def one(x, carry):
            for y in range(ny):
                v = own[x, y : y + 1, :]
                at = pl.ds(pl.multiple_of((x * ny + y) * nz, nz), nz)
                low = jnp.broadcast_to((v & (nz - 1)).astype(F32), (16, nz)).astype(BF16)
                high = jnp.broadcast_to((v >> 7).astype(F32), (16, nz)).astype(BF16)
                for k in range(nz // 16):
                    lo_hot[16 * k : 16 * k + 16, at] = jnp.where(bands[k] == low, yes, no)
                for k in range(groups // 16):
                    hi_hot[16 * k : 16 * k + 16, at] = jnp.where(bands[k] == high, yes, no)
            return carry

        lax.fori_loop(x0, x1, one, 0, unroll=True)

    loads[3].wait()
    loads[4].wait()
    for s in range(SWEEPS):
        local(s)
        hots(s * nx // SWEEPS, (s + 1) * nx // SWEEPS)
        for i in range(3):
            wait_recv(functools.partial(face, s), i)
        accs = finish(s, range(nx), None)
        if s < SWEEPS - 1:
            start(functools.partial(face, s + 1), 0)
            for g in range(2):
                sz[s + 1, g] = accs[g]
            start(functools.partial(face, s + 1), 2)
            pack_y(f.at[s], s + 1)
            start(functools.partial(face, s + 1), 1)

    def plane(x, total):
        sens = jnp.zeros((ny, nz), F32)
        for k in range(pairs // 2):
            fr, fi = out[2 * k, x], out[2 * k + 1, x]
            gr, gi = out[pairs + 2 * k, x], out[pairs + 2 * k + 1, x]
            sens = sens + (fr * gi + fi * gr)
        sens = ab[2, x] * sens
        s0 = sens.astype(BF16).astype(F32)
        rest = sens - s0
        s1 = rest.astype(BF16).astype(F32)
        s2 = rest - s1
        left = []
        for piece in (s0, s1, s2):
            row = jnp.concatenate(
                [jnp.broadcast_to(piece[y : y + 1, :], (groups, nz)) for y in range(ny)], 1
            ).astype(BF16)
            left.append(row)
        at = pl.ds(pl.multiple_of(x * ny * nz, nz), ny * nz)
        hi = hi_hot[:, at]
        lhs = jnp.concatenate([hi * row for row in left], 0)
        return total + lax.dot_general(
            lhs, lo_hot[:, at], (((1,), (1,)), ((), ())), preferred_element_type=F32
        )

    total = lax.fori_loop(0, nx, plane, jnp.zeros((3 * groups, nz), F32), unroll=True)
    part[...] = total[:groups] + total[groups : 2 * groups] + total[2 * groups :]

    rows = groups // n

    def rs_copy(d):
        return pltpu.make_async_remote_copy(
            src_ref=part.at[pl.ds(pl.multiple_of(peers[d - 1] * rows, rows), rows)],
            dst_ref=rs.at[d - 1],
            send_sem=rsend.at[d - 1],
            recv_sem=rrecv.at[d - 1],
            device_id={"gz": peers[d - 1]},
            device_id_type=MESH,
        )

    for d in range(1, n):
        rs_copy(d).start()

    for i in range(3):
        wait_recv(model_copy, i)
    m = mod[...]
    mz = m.shape[2]
    mlane = lax.broadcasted_iota(jnp.int32, m.shape, 2)
    total = jnp.concatenate([hm[0][-1:], m[:-1]], 0) + jnp.concatenate([m[1:], hm[1][:1]], 0)
    total = total + jnp.concatenate([hm[2][:, -1:], m[:, :-1]], 1)
    total = total + jnp.concatenate([m[:, 1:], hm[3][:, :1]], 1)
    total = total + pltpu.roll(jnp.where(mlane == mz - 1, hm[4], m), 1, 2)
    total = total + pltpu.roll(jnp.where(mlane == 0, hm[5], m), mz - 1, 2)
    smooth = 6.0 * m - total

    owned = part[pl.ds(pl.multiple_of(pos[2] * rows, rows), rows), :]
    for d in range(1, n):
        rs_copy(d).wait_recv()
    for d in range(1, n):
        owned = owned + rs[d - 1]
    my = m.shape[1]
    for k in range(m.shape[0]):
        grad[k] = owned[k * my : (k + 1) * my] + smooth[k]

    for s in range(SWEEPS):
        for i in range(3):
            wait_send(functools.partial(face, s), i)
    for i in range(3):
        wait_send(model_copy, i)
    for d in range(1, n):
        rs_copy(d).wait_send()


def solution(mesh):
    sizes = tuple(mesh.shape[a] for a in AXES)

    def body(initial, source, classes, coupling, owner, model):
        chans, nx, ny, nz = initial.shape
        n = sizes[2]
        groups = n * model.size // nz
        dma = pltpu.SemaphoreType.DMA
        vmem = pl.BlockSpec(memory_space=pltpu.VMEM)
        hbm = pl.BlockSpec(memory_space=pltpu.HBM)
        return pl.pallas_call(
            functools.partial(kernel, sizes),
            out_shape=(
                jax.ShapeDtypeStruct(initial.shape, F32),
                jax.ShapeDtypeStruct(model.shape, F32),
            ),
            in_specs=[hbm, hbm, hbm, pl.BlockSpec(memory_space=pltpu.SMEM), hbm, hbm],
            out_specs=(vmem, vmem),
            scratch_shapes=[
                pltpu.VMEM(initial.shape, F32),
                pltpu.VMEM(source.shape, F32),
                pltpu.VMEM(classes.shape, jnp.int32),
                pltpu.VMEM(owner.shape, jnp.int32),
                pltpu.VMEM(model.shape, F32),
                pltpu.VMEM((SWEEPS - 1, chans, nx, ny, nz), F32),
                pltpu.VMEM((chans, nx, ny, nz), F32),
                pltpu.VMEM((chans, nx, ny, nz), F32),
                pltpu.VMEM((3, nx, ny, nz), F32),
                pltpu.VMEM((SWEEPS, 2, chans, ny, nz), F32),
                pltpu.VMEM((SWEEPS, 2, chans, nx, nz), F32),
                pltpu.VMEM((SWEEPS, 2, 2, ny, nz), F32),
                pltpu.VMEM((SWEEPS, 2, chans, nx, nz), F32),
                pltpu.VMEM((SWEEPS, 2, ny, nz), F32),
                pltpu.VMEM((6,) + model.shape, F32),
                pltpu.VMEM((nz, nx * ny * nz), BF16),
                pltpu.VMEM((groups, nx * ny * nz), BF16),
                pltpu.VMEM((groups, nz), F32),
                pltpu.VMEM((n - 1, groups // n, nz), F32),
                dma((5,)),
                dma((SWEEPS, 6)),
                dma((SWEEPS, 6)),
                dma((6,)),
                dma((6,)),
                dma((n - 1,)),
                dma((n - 1,)),
            ],
            compiler_params=pltpu.CompilerParams(
                collective_id=0, has_side_effects=True, vmem_limit_bytes=60 * 1024 * 1024
            ),
        )(initial, source, classes, coupling, owner, model)

    in_specs = (
        P(None, "gx", "gy", "gz"),
        P(None, "gx", "gy", "gz"),
        P("gx", "gy", "gz"),
        P(),
        P("gx", "gy", "gz"),
        P("gx", "gy", "gz"),
    )
    out_specs = (P(None, "gx", "gy", "gz"), P("gx", "gy", "gz"))
    return jax.shard_map(body, mesh=mesh, in_specs=in_specs, out_specs=out_specs, check_vma=False)
```

profile of v0, /device:TPU:0, one launch (start us, length us, event | category | flops | bytes accessed | tf_op | source)
XLA Modules:
  0.0 28.1 jit_solution(2740401123860987702)
XLA Ops:
  0.6 25.1 %shard_map.77 = (f32[12,8,8,128]{3,2,1,0:T(8,128)}, f32[2,4,128]{2,1,0:T(4,128)}) custom-call(f32[12,8,8,128]{3,2,1,0:T(8,128)} %init_hbm.1, f32[12,8,8,128]{3,2,1,0:T(8,128)} %src_hbm.1, s32[8,8,128]{2,1,0:T(8,128)} %cls_hbm.1, f32[16]{0:T(128)} %coup.1, s32[8,8,128]{2,1,0:T(8,128)} %own_hbm.1, f32[2,4,128]{2,1,0:T(4,128)} %mod_hbm.1), custom_call_target="tpu_custom_call" | custom-call | tf_op jit(solution)/shard_map/pallas_call | solution.py:347
  25.7 0.0 copy-start
  25.7 1.8 %copy.10 = f32[12,8,8,128]{3,2,1,0:T(8,128)} copy(f32[12,8,8,128]{3,2,1,0:T(8,128)} %get-tuple-element.4) | data formatting | bytes 786432
  27.5 0.0 copy-done
  27.5 0.6 %copy.11 = f32[2,4,128]{2,1,0:T(4,128)} copy(f32[2,4,128]{2,1,0:T(4,128)S(1)} %copy-done) | data formatting | bytes 8192
Async XLA Ops:
  25.7 1.8 %copy-start = (f32[2,4,128]{2,1,0:T(4,128)S(1)}, f32[2,4,128]{2,1,0:T(4,128)}, u32[]{:S(2)}) copy-start(f32[2,4,128]{2,1,0:T(4,128)} %get-tuple-element.5) | copy-start | bytes 12292
where the time goes:
time: 28.3 us; the launch traced here: 28.1 us
  Pallas kernels  25.1 us (89%)
  local copies, waits for them, and re-layouts  2.36 us (8%)
  between operations  0.65 us (2%)
    pallas_call x1, Pallas kernels, body(): pl.pallas_call(functools.partial(kernel, sizes), out_shape=(jax.ShapeDtyp...  25.1 us
    unnamed x4, local copies, waits for them, and re-layouts  2.36 us

commit v1 on v0

--- a/solution.py
+++ b/solution.py
@@ -334,6 +334,17 @@
         rs_copy(d).wait_send()
 
 
+def flush(fields, grad, fields_hbm, grad_hbm, sem):
+    copies = [
+        pltpu.make_async_copy(fields, fields_hbm, sem.at[0]),
+        pltpu.make_async_copy(grad, grad_hbm, sem.at[1]),
+    ]
+    for copy in copies:
+        copy.start()
+    for copy in copies:
+        copy.wait()
+
+
 def solution(mesh):
     sizes = tuple(mesh.shape[a] for a in AXES)
 
@@ -344,11 +355,11 @@
         dma = pltpu.SemaphoreType.DMA
         vmem = pl.BlockSpec(memory_space=pltpu.VMEM)
         hbm = pl.BlockSpec(memory_space=pltpu.HBM)
-        return pl.pallas_call(
+        results = pl.pallas_call(
             functools.partial(kernel, sizes),
             out_shape=(
-                jax.ShapeDtypeStruct(initial.shape, F32),
-                jax.ShapeDtypeStruct(model.shape, F32),
+                pltpu.VMEM(initial.shape, F32),
+                pltpu.VMEM(model.shape, F32),
             ),
             in_specs=[hbm, hbm, hbm, pl.BlockSpec(memory_space=pltpu.SMEM), hbm, hbm],
             out_specs=(vmem, vmem),
@@ -384,6 +395,16 @@
                 collective_id=0, has_side_effects=True, vmem_limit_bytes=60 * 1024 * 1024
             ),
         )(initial, source, classes, coupling, owner, model)
+        return pl.pallas_call(
+            flush,
+            out_shape=(
+                jax.ShapeDtypeStruct(initial.shape, F32),
+                jax.ShapeDtypeStruct(model.shape, F32),
+            ),
+            in_specs=[vmem, vmem],
+            out_specs=(hbm, hbm),
+            scratch_shapes=[dma((2,))],
+        )(*[pltpu.with_memory_space_constraint(r, pltpu.VMEM) for r in results])
 
     in_specs = (
         P(None, "gx", "gy", "gz"),

time: 28.3 us -> 25.9 us (0.915)
  local copies, waits for them, and re-layouts: 2.36 us -> 0 us
    unnamed x4 -> x0, local copies, waits for them, and re-layouts: 2.36 us -> none
    pallas_call x1 -> x2, Pallas kernels: 25.1 us -> 25.1 us  [the longest x1 24.3 us: body(): pl.pallas_call(functools.partial(kernel, sizes), out_shape=(pltpu.VMEM(in...]
where the time goes in v1:
time: 25.9 us; the launch traced here: 25.8 us
  Pallas kernels  25.1 us (97%)
  between operations  0.64 us (2%)
    pallas_call x1, Pallas kernels, body(): pl.pallas_call(functools.partial(kernel, sizes), out_shape=(pltpu.VMEM(in...  24.3 us
    pallas_call x1, Pallas kernels, body(): pl.pallas_call(flush, out_shape=(jax.ShapeDtypeStruct(initial.shape, F32)...  0.77 us

profile of v1, /device:TPU:0, one launch (start us, length us, event | category | flops | bytes accessed | tf_op | source)
XLA Modules:
  0.0 25.8 jit_solution(1696475681129943276)
XLA Ops:
  0.6 24.3 %shard_map.77 = (f32[12,8,8,128]{3,2,1,0:T(8,128)S(1)}, f32[2,4,128]{2,1,0:T(4,128)S(1)}) custom-call(f32[12,8,8,128]{3,2,1,0:T(8,128)} %init_hbm.1, f32[12,8,8,128]{3,2,1,0:T(8,128)} %src_hbm.1, s32[8,8,128]{2,1,0:T(8,128)} %cls_hbm.1, f32[16]{0:T(128)} %coup.1, s32[8,8,128]{2,1,0:T(8,128)} %own_hbm.1, f32[2,4,128]{2,1,0:T(4,128)} %mod_hbm.1), custom_call_target="tpu_custom_call" | custom-call | tf_op jit(solution)/shard_map/pallas_call | solution.py:358
  25.0 0.8 %shard_map.78 = (f32[12,8,8,128]{3,2,1,0:T(8,128)}, f32[2,4,128]{2,1,0:T(4,128)}) custom-call(f32[12,8,8,128]{3,2,1,0:T(8,128)S(1)} %get-tuple-element.4.fields, f32[2,4,128]{2,1,0:T(4,128)S(1)} %get-tuple-element.5.grad), custom_call_target="tpu_custom_call" | custom-call | tf_op jit(solution)/shard_map/pallas_call | solution.py:398

commit v2 on v1

--- a/solution.py
+++ b/solution.py
@@ -15,12 +15,13 @@
 
 
 def kernel(
-    sizes, init_hbm, src_hbm, cls_hbm, coup, own_hbm, mod_hbm, out, grad,
-    init, src, cls, own, mod, f, part_next, const, ab, hx, hy, hz, sy, sz, hm, lo_hot, hi_hot, part, rs,
+    sizes, init_hbm, src_hbm, cls_hbm, coup_hbm, own_hbm, mod_hbm, out, grad,
+    init, src, cls, coup, own, mod, f, part_next, const, ab, ycor, hx, hy, hz, sy, sz, hm, lo_hot, hi_hot, part, rs,
     load_sem, send_sem, recv_sem, msend, mrecv, rsend, rrecv,
 ):
     chans, nx, ny, nz = init.shape
     pairs = chans // 2
+    half = chans // 2
     per_vreg = chans * nx // 2
     pos = [lax.axis_index(a) for a in AXES]
     has = [(pos[i] > 0, pos[i] < sizes[i] - 1) for i in range(3)]
@@ -50,6 +51,7 @@
         for k, (a, b) in enumerate(
             (
                 (init_hbm, init), (mod_hbm, mod), (cls_hbm, cls), (src_hbm, src), (own_hbm, own),
+                (coup_hbm, coup),
             )
         )
     ]
@@ -57,9 +59,6 @@
         load.start()
 
     lane = lax.broadcasted_iota(jnp.int32, (ny, nz), 1)
-    sub = lax.broadcasted_iota(jnp.int32, (ny, nz), 0)
-    lane3 = lax.broadcasted_iota(jnp.int32, (nx, ny, nz), 2)
-    sub3 = lax.broadcasted_iota(jnp.int32, (nx, ny, nz), 1)
 
     for i, halo in enumerate((hx, hy, hz)):
         for side in range(2):
@@ -69,22 +68,23 @@
                 halo[:, side] = jnp.zeros((SWEEPS,) + halo.shape[2:], F32)
                 hm[2 * i + side] = jnp.zeros(hm.shape[1:], F32)
 
-    def face(s, i, side):
+    def face(s, g, i, side):
         cells = init if s == 0 else f.at[s - 1]
+        mine = pl.ds(g * half, half)
         if i == 0:
-            source = cells.at[:, 0 if side == 0 else nx - 1]
-            halo = hx
+            source = cells.at[mine, 0 if side == 0 else nx - 1]
+            halo = hx.at[s, 1 - side, mine]
         elif i == 1:
-            source = sy.at[s, side]
-            halo = hy
+            source = sy.at[s, side, mine]
+            halo = hy.at[s, 1 - side, mine]
         else:
-            source = sz.at[s]
-            halo = hz
+            source = sz.at[s, g]
+            halo = hz.at[s, 1 - side, g]
         return pltpu.make_async_remote_copy(
             src_ref=source,
-            dst_ref=halo.at[s, 1 - side],
-            send_sem=send_sem.at[s, 2 * i + side],
-            recv_sem=recv_sem.at[s, 2 * i + 1 - side],
+            dst_ref=halo,
+            send_sem=send_sem.at[s, g, 2 * i + side],
+            recv_sem=recv_sem.at[s, g, 2 * i + 1 - side],
             device_id={AXES[i]: ends[i][side]},
             device_id_type=MESH,
         )
@@ -120,9 +120,9 @@
             def _():
                 make(i, side).wait_send()
 
-    def pack_y(cells, s):
+    def pack_y(cells, s, g):
         flat = cells.reshape(chans * nx * ny, nz)
-        for c in range(chans):
+        for c in range(g * half, g * half + half):
             for side, row in ((0, 0), (1, ny - 1)):
                 sy[s, side, c] = flat[pl.ds(c * nx * ny + row, nx, stride=ny), :]
 
@@ -130,8 +130,8 @@
         return jnp.where((lane >> 1) == j, pltpu.roll(value, 2 * j + 1, 1), acc)
 
     loads[0].wait()
-    pack_y(init, 0)
     for g in range(2):
+        pack_y(init, 0, g)
         acc = jnp.zeros((ny, nz), F32)
         for j in range(per_vreg):
             c, x = divmod(g * per_vreg + j, nx)
@@ -139,13 +139,15 @@
         sz[0, g] = acc
 
     pl.semaphore_wait(barrier, greeted)
-    for i in range(3):
-        start(functools.partial(face, 0), i)
+    for g in range(2):
+        for i in (1, 2, 0):
+            start(functools.partial(face, 0, g), i)
     loads[1].wait()
     for i in range(3):
         start(model_copy, i)
 
     loads[2].wait()
+    loads[5].wait()
     classes = cls[...]
     kappa = jnp.zeros(classes.shape, F32)
     for k in range(coup.shape[0]):
@@ -158,12 +160,10 @@
     def shifted(v):
         zero = jnp.zeros((1, ny, nz), F32)
         total = jnp.concatenate([zero, v[:-1]], 0) + jnp.concatenate([v[1:], zero], 0)
-        total = total + jnp.where(sub3 == 0, 0.0, pltpu.roll(v, 1, 1))
-        total = total + jnp.where(sub3 == ny - 1, 0.0, pltpu.roll(v, ny - 1, 1))
-        total = total + jnp.where(lane3 == 0, 0.0, pltpu.roll(v, 1, 2))
-        return total + jnp.where(lane3 == nz - 1, 0.0, pltpu.roll(v, nz - 1, 2))
-
-    def local(s):
+        total = total + (pltpu.roll(v, 1, 1) + pltpu.roll(v, ny - 1, 1))
+        return total + (pltpu.roll(v, 1, 2) + pltpu.roll(v, nz - 1, 2))
+
+    def local(s, g):
         cells = init if s == 0 else f.at[s - 1]
 
         def one(p, carry):
@@ -181,49 +181,48 @@
             part_next[2 * p + 1] = ci + 0.2 * fi + (a * ti - b * tr)
             return carry
 
-        lax.fori_loop(0, pairs, one, 0, unroll=True)
-
-    def finish(s, planes, accs):
-        results = []
+        lax.fori_loop(g * pairs // 2, (g + 1) * pairs // 2, one, 0, unroll=True)
+
+    ycor[...] = jnp.zeros(ycor.shape, F32)
+
+    def finish(s, g):
         cells = out if s == SWEEPS - 1 else f.at[s]
         last = s == SWEEPS - 1
-        merged = [
-            jnp.where((lane & 1) == 0, hz[s, 0, g], pltpu.roll(hz[s, 1, g], nz - 2, 1))
-            for g in range(2)
-        ]
+        own_z = sz[s, g]
+        merged = jnp.where(
+            (lane & 1) == 0, hz[s, 0, g] - own_z, pltpu.roll(hz[s, 1, g] - own_z, nz - 2, 1)
+        )
         edge = (lane == 0) | (lane == nz - 1)
-
-        for g in range(2):
-
-            def one(q, acc):
-                for x in planes:
-                    sums = []
-                    for r in range(2):
-                        c = g * (chans // 2) + 2 * q + r
-                        j = (2 * q + r) * nx + x
-                        low = jnp.broadcast_to(hy[s, 0, c, x : x + 1, :], (ny, nz))
-                        high = jnp.broadcast_to(hy[s, 1, c, x : x + 1, :], (ny, nz))
-                        h = jnp.where(sub == 0, low, jnp.where(sub == ny - 1, high, 0.0))
-                        h = h + jnp.where(edge, pltpu.roll(merged[g], nz - 2 * j, 1), 0.0)
-                        if x == 0:
-                            h = h + hx[s, 0, c]
-                        if x == nx - 1:
-                            h = h + hx[s, 1, c]
-                        sums.append(h)
-                    a, b = ab[0, x], ab[1, x]
-                    c = g * (chans // 2) + 2 * q
-                    nr = part_next[c, x] + (a * sums[0] + b * sums[1])
-                    ni = part_next[c + 1, x] + (a * sums[1] - b * sums[0])
-                    cells[c, x] = nr
-                    cells[c + 1, x] = ni
-                    if not last:
-                        acc = pack_z(acc, nr, 2 * q * nx + x)
-                        acc = pack_z(acc, ni, (2 * q + 1) * nx + x)
-                return acc
-
-            first = jnp.zeros((ny, nz), F32) if accs is None else accs[g]
-            results.append(lax.fori_loop(0, pairs // 2, one, first, unroll=True))
-        return results
+        rows = ycor.reshape(chans * nx * ny, nz)
+        for c in range(g * half, g * half + half):
+            for side, row in ((0, 0), (1, ny - 1)):
+                rows[pl.ds(c * nx * ny + row, nx, stride=ny), :] = (
+                    hy[s, side, c] - sy[s, 1 - side, c]
+                )
+
+        def one(q, acc):
+            c = g * half + 2 * q
+            for x in range(nx):
+                sums = []
+                for r in range(2):
+                    j = (2 * q + r) * nx + x
+                    h = ycor[c + r, x] + jnp.where(edge, pltpu.roll(merged, nz - 2 * j, 1), 0.0)
+                    if x == 0:
+                        h = h + hx[s, 0, c + r]
+                    if x == nx - 1:
+                        h = h + hx[s, 1, c + r]
+                    sums.append(h)
+                a, b = ab[0, x], ab[1, x]
+                nr = part_next[c, x] + (a * sums[0] + b * sums[1])
+                ni = part_next[c + 1, x] + (a * sums[1] - b * sums[0])
+                cells[c, x] = nr
+                cells[c + 1, x] = ni
+                if not last:
+                    acc = pack_z(acc, nr, 2 * q * nx + x)
+                    acc = pack_z(acc, ni, (2 * q + 1) * nx + x)
+            return acc
+
+        return lax.fori_loop(0, pairs // 2, one, jnp.zeros((ny, nz), F32), unroll=True)
 
     groups = hi_hot.shape[0]
 
@@ -248,19 +247,22 @@
 
     loads[3].wait()
     loads[4].wait()
+    for g in range(2):
+        local(0, g)
+    hots(0, nx // SWEEPS)
     for s in range(SWEEPS):
-        local(s)
-        hots(s * nx // SWEEPS, (s + 1) * nx // SWEEPS)
-        for i in range(3):
-            wait_recv(functools.partial(face, s), i)
-        accs = finish(s, range(nx), None)
+        for g in range(2):
+            for i in (0, 2, 1):
+                wait_recv(functools.partial(face, s, g), i)
+            packed = finish(s, g)
+            if s < SWEEPS - 1:
+                sz[s + 1, g] = packed
+                pack_y(f.at[s], s + 1, g)
+                for i in (1, 2, 0):
+                    start(functools.partial(face, s + 1, g), i)
+                local(s + 1, g)
         if s < SWEEPS - 1:
-            start(functools.partial(face, s + 1), 0)
-            for g in range(2):
-                sz[s + 1, g] = accs[g]
-            start(functools.partial(face, s + 1), 2)
-            pack_y(f.at[s], s + 1)
-            start(functools.partial(face, s + 1), 1)
+            hots((s + 1) * nx // SWEEPS, (s + 2) * nx // SWEEPS)
 
     def plane(x, total):
         sens = jnp.zeros((ny, nz), F32)
@@ -326,8 +328,9 @@
         grad[k] = owned[k * my : (k + 1) * my] + smooth[k]
 
     for s in range(SWEEPS):
-        for i in range(3):
-            wait_send(functools.partial(face, s), i)
+        for g in range(2):
+            for i in range(3):
+                wait_send(functools.partial(face, s, g), i)
     for i in range(3):
         wait_send(model_copy, i)
     for d in range(1, n):
@@ -361,18 +364,20 @@
                 pltpu.VMEM(initial.shape, F32),
                 pltpu.VMEM(model.shape, F32),
             ),
-            in_specs=[hbm, hbm, hbm, pl.BlockSpec(memory_space=pltpu.SMEM), hbm, hbm],
+            in_specs=[hbm] * 6,
             out_specs=(vmem, vmem),
             scratch_shapes=[
                 pltpu.VMEM(initial.shape, F32),
                 pltpu.VMEM(source.shape, F32),
                 pltpu.VMEM(classes.shape, jnp.int32),
+                pltpu.SMEM(coupling.shape, F32),
                 pltpu.VMEM(owner.shape, jnp.int32),
                 pltpu.VMEM(model.shape, F32),
                 pltpu.VMEM((SWEEPS - 1, chans, nx, ny, nz), F32),
                 pltpu.VMEM((chans, nx, ny, nz), F32),
                 pltpu.VMEM((chans, nx, ny, nz), F32),
                 pltpu.VMEM((3, nx, ny, nz), F32),
+                pltpu.VMEM((chans, nx, ny, nz), F32),
                 pltpu.VMEM((SWEEPS, 2, chans, ny, nz), F32),
                 pltpu.VMEM((SWEEPS, 2, chans, nx, nz), F32),
                 pltpu.VMEM((SWEEPS, 2, 2, ny, nz), F32),
@@ -383,9 +388,9 @@
                 pltpu.VMEM((groups, nx * ny * nz), BF16),
                 pltpu.VMEM((groups, nz), F32),
                 pltpu.VMEM((n - 1, groups // n, nz), F32),
-                dma((5,)),
-                dma((SWEEPS, 6)),
-                dma((SWEEPS, 6)),
+                dma((6,)),
+                dma((SWEEPS, 2, 6)),
+                dma((SWEEPS, 2, 6)),
                 dma((6,)),
                 dma((6,)),
                 dma((n - 1,)),

time: 25.9 us -> 24.9 us (0.961)
  Pallas kernels: 25.1 us -> 24.2 us
    pallas_call x1, Pallas kernels: 24.3 us -> 23.4 us  [body(): pl.pallas_call(functools.partial(kernel, sizes), out_shape=(pltpu.VMEM(in...]
where the time goes in v2:
time: 24.9 us; the launch traced here: 24.8 us
  Pallas kernels  24.2 us (97%)
  between operations  0.64 us (3%)
    pallas_call x1, Pallas kernels, body(): pl.pallas_call(functools.partial(kernel, sizes), out_shape=(pltpu.VMEM(in...  23.4 us
    pallas_call x1, Pallas kernels, body(): pl.pallas_call(flush, out_shape=(jax.ShapeDtypeStruct(initial.shape, F32)...  0.77 us

profile of v2, /device:TPU:0, one launch (start us, length us, event | category | flops | bytes accessed | tf_op | source)
XLA Modules:
  0.0 24.8 jit_solution(18327543757076935362)
XLA Ops:
  0.6 23.4 %shard_map.77 = (f32[12,8,8,128]{3,2,1,0:T(8,128)S(1)}, f32[2,4,128]{2,1,0:T(4,128)S(1)}) custom-call(f32[12,8,8,128]{3,2,1,0:T(8,128)} %init_hbm.1, f32[12,8,8,128]{3,2,1,0:T(8,128)} %src_hbm.1, s32[8,8,128]{2,1,0:T(8,128)} %cls_hbm.1, f32[16]{0:T(128)} %coup_hbm.1, s32[8,8,128]{2,1,0:T(8,128)} %own_hbm.1, f32[2,4,128]{2,1,0:T(4,128)} %mod_hbm.1), custom_call_target="tpu_custom_call" | custom-call | tf_op jit(solution)/shard_map/pallas_call | solution.py:361
  24.0 0.8 %shard_map.78 = (f32[12,8,8,128]{3,2,1,0:T(8,128)}, f32[2,4,128]{2,1,0:T(4,128)}) custom-call(f32[12,8,8,128]{3,2,1,0:T(8,128)S(1)} %get-tuple-element.4.fields, f32[2,4,128]{2,1,0:T(4,128)S(1)} %get-tuple-element.5.grad), custom_call_target="tpu_custom_call" | custom-call | tf_op jit(solution)/shard_map/pallas_call | solution.py:403

commit v3 on v2

--- a/solution.py
+++ b/solution.py
@@ -16,8 +16,10 @@
 
 def kernel(
     sizes, init_hbm, src_hbm, cls_hbm, coup_hbm, own_hbm, mod_hbm, out, grad,
-    init, src, cls, coup, own, mod, f, part_next, const, ab, ycor, hx, hy, hz, sy, sz, hm, lo_hot, hi_hot, part, rs,
-    load_sem, send_sem, recv_sem, msend, mrecv, rsend, rrecv,
+    init, src, cls, coup, own, mod, f, part_next, const, kap, ycor,
+    hx, hy, hy2, hz, hxy, hxz, hyz, hcx, hcy, hcz, sy, sy2, sz, sxy, scy, scz,
+    hm, lo_hot, hi_hot, part, rs,
+    load_sem, send_sem, recv_sem, esend, erecv, csend, crecv, msend, mrecv, rsend, rrecv,
 ):
     chans, nx, ny, nz = init.shape
     pairs = chans // 2
@@ -28,6 +30,12 @@
     n = sizes[2]
     peers = [lax.rem(pos[2] + d, n) for d in range(1, n)]
     ends = [[pos[i] - 1, pos[i] + 1] for i in range(3)]
+    lines = [
+        (m, i, j, si, sj)
+        for m, (i, j) in enumerate(((0, 1), (0, 2), (1, 2)))
+        for si in range(2)
+        for sj in range(2)
+    ]
 
     barrier = pltpu.get_barrier_semaphore()
     for i in range(2):
@@ -41,10 +49,27 @@
 
     for d in range(1, n):
         pl.semaphore_signal(barrier, inc=1, device_id={"gz": peers[d - 1]}, device_id_type=MESH)
+
+    def met(i, j, si, sj):
+        return jnp.logical_and(has[i][si], has[j][sj])
+
+    for m, i, j, si, sj in lines:
+
+        @pl.when(met(i, j, si, sj))
+        def _():
+            pl.semaphore_signal(
+                barrier,
+                inc=1,
+                device_id={AXES[i]: ends[i][si], AXES[j]: ends[j][sj]},
+                device_id_type=MESH,
+            )
+
     greeted = n - 1
     for i in range(2):
         for side in range(2):
             greeted = greeted + has[i][side].astype(jnp.int32)
+    for m, i, j, si, sj in lines:
+        greeted = greeted + met(i, j, si, sj).astype(jnp.int32)
 
     loads = [
         pltpu.make_async_copy(a, b, load_sem.at[k])
@@ -59,32 +84,101 @@
         load.start()
 
     lane = lax.broadcasted_iota(jnp.int32, (ny, nz), 1)
+    sub = lax.broadcasted_iota(jnp.int32, (ny, nz), 0)
+    even = (lane & 1) == 0
+    shift3 = jnp.where(even, lane, lane - 3)
+    xlane = (lane >> 1) % nx
+    real = ((lane // (2 * nx)) & 1) == 0
 
     for i, halo in enumerate((hx, hy, hz)):
         for side in range(2):
 
             @pl.when(jnp.logical_not(has[i][side]))
             def _():
-                halo[:, side] = jnp.zeros((SWEEPS,) + halo.shape[2:], F32)
+                halo[:, side] = jnp.zeros(halo.shape[:1] + halo.shape[2:], F32)
                 hm[2 * i + side] = jnp.zeros(hm.shape[1:], F32)
 
-    def face(s, g, i, side):
-        cells = init if s == 0 else f.at[s - 1]
+    held = (hxy, hxz, hyz)
+    for m, i, j, si, sj in lines:
+
+        @pl.when(jnp.logical_not(met(i, j, si, sj)))
+        def _():
+            line = held[m]
+            line[:, 2 * si + sj] = jnp.zeros(line.shape[:1] + line.shape[2:], F32)
+
+    def face(e, g, i, side):
+        s = 2 * e
+        cells = init if e == 0 else f.at[s - 1]
         mine = pl.ds(g * half, half)
+        axis = i
         if i == 0:
-            source = cells.at[mine, 0 if side == 0 else nx - 1]
+            source = cells.at[mine, pl.ds(0 if side == 0 else nx - 2, 2)]
             halo = hx.at[s, 1 - side, mine]
         elif i == 1:
             source = sy.at[s, side, mine]
             halo = hy.at[s, 1 - side, mine]
-        else:
+        elif i == 2:
             source = sz.at[s, g]
             halo = hz.at[s, 1 - side, g]
+        else:
+            axis = 1
+            source = sy2.at[e, side, mine]
+            halo = hy2.at[e, 1 - side, mine]
         return pltpu.make_async_remote_copy(
             src_ref=source,
             dst_ref=halo,
-            send_sem=send_sem.at[s, g, 2 * i + side],
-            recv_sem=recv_sem.at[s, g, 2 * i + 1 - side],
+            send_sem=send_sem.at[e, g, 2 * i + side],
+            recv_sem=recv_sem.at[e, g, 2 * i + 1 - side],
+            device_id={AXES[axis]: ends[axis][side]},
+            device_id_type=MESH,
+        )
+
+    def line_copy(e, m, i, j, si, sj):
+        s = 2 * e
+        source = (sxy.at[e, 2 * si + sj], sz.at[s, :, 0], sz.at[s, :, pl.ds(0, 2)])[m]
+        there = 2 * (1 - si) + 1 - sj
+        return pltpu.make_async_remote_copy(
+            src_ref=source,
+            dst_ref=held[m].at[e, there],
+            send_sem=esend.at[e, 4 * m + 2 * si + sj],
+            recv_sem=erecv.at[e, 4 * m + there],
+            device_id={AXES[i]: ends[i][si], AXES[j]: ends[j][sj]},
+            device_id_type=MESH,
+        )
+
+    def start_lines(e):
+        for m, i, j, si, sj in lines:
+
+            @pl.when(met(i, j, si, sj))
+            def _():
+                line_copy(e, m, i, j, si, sj).start()
+
+    def wait_lines(e):
+        for m, i, j, si, sj in lines:
+
+            @pl.when(met(i, j, si, sj))
+            def _():
+                line_copy(e, m, i, j, 1 - si, 1 - sj).wait_recv()
+
+    def wait_lines_sent(e):
+        for m, i, j, si, sj in lines:
+
+            @pl.when(met(i, j, si, sj))
+            def _():
+                line_copy(e, m, i, j, si, sj).wait_send()
+
+    def const_copy(i, side):
+        if i == 0:
+            source, halo = const.at[:, 0 if side == 0 else nx - 1], hcx
+        elif i == 1:
+            source, halo = scy.at[side], hcy
+        else:
+            source, halo = scz, hcz
+        return pltpu.make_async_remote_copy(
+            src_ref=source,
+            dst_ref=halo.at[1 - side],
+            send_sem=csend.at[2 * i + side],
+            recv_sem=crecv.at[2 * i + 1 - side],
             device_id={AXES[i]: ends[i][side]},
             device_id_type=MESH,
         )
@@ -102,46 +196,85 @@
     def start(make, i):
         for side in range(2):
 
-            @pl.when(has[i][side])
+            @pl.when(has[i % 2 if i == 3 else i][side])
             def _():
                 make(i, side).start()
 
     def wait_recv(make, i):
         for side in range(2):
 
-            @pl.when(has[i][side])
+            @pl.when(has[i % 2 if i == 3 else i][side])
             def _():
                 make(i, 1 - side).wait_recv()
 
     def wait_send(make, i):
         for side in range(2):
 
-            @pl.when(has[i][side])
+            @pl.when(has[i % 2 if i == 3 else i][side])
             def _():
                 make(i, side).wait_send()
 
-    def pack_y(cells, s, g):
-        flat = cells.reshape(chans * nx * ny, nz)
-        for c in range(g * half, g * half + half):
-            for side, row in ((0, 0), (1, ny - 1)):
-                sy[s, side, c] = flat[pl.ds(c * nx * ny + row, nx, stride=ny), :]
+    def rows_of(cells, into, channels, rows):
+        flat = cells.reshape(cells.shape[0] * nx * ny, nz)
+        for c in channels:
+            for side, row in enumerate(rows):
+                into[side, c] = flat[pl.ds(c * nx * ny + row, nx, stride=ny), :]
+
+    def channels_of(g):
+        return range(g * half, g * half + half)
 
     def pack_z(acc, value, j):
         return jnp.where((lane >> 1) == j, pltpu.roll(value, 2 * j + 1, 1), acc)
 
+    def pack_z2(acc, value, j):
+        return jnp.where(shift3 == 2 * j, pltpu.roll(value, 2 * j + 2, 1), acc)
+
+    def pack_rows(cells, s, g):
+        rows_of(cells, sy.at[s], channels_of(g), (0, ny - 1))
+
+    def pack_exchange(cells, e, g):
+        s = 2 * e
+        pack_rows(cells, s, g)
+        rows_of(cells, sy2.at[e], channels_of(g), (1, ny - 2))
+        acc = jnp.zeros((nx, nz), F32)
+        for k in range(half):
+            for side in range(2):
+                acc = pack_z(acc, sy[s, side, g * half + k], 2 * k + side)
+        sz[s, g, 1] = acc
+
+    def pack_corners(e):
+        for side in range(2):
+            flat = sy.at[2 * e, side].reshape(chans * nx, nz)
+            for end, x in enumerate((0, nx - 1)):
+                sxy[e, 2 * end + side, 0:chans] = flat[pl.ds(x, chans, stride=nx), :]
+
+    def send_exchange(e, g):
+        for i in (1, 2, 0):
+            start(functools.partial(face, e, g), i)
+
+    def send_rest(e):
+        for g in range(2):
+            start(functools.partial(face, e, g), 3)
+        start_lines(e)
+
     loads[0].wait()
     for g in range(2):
-        pack_y(init, 0, g)
+        pack_exchange(init, 0, g)
         acc = jnp.zeros((ny, nz), F32)
+        acc2 = jnp.zeros((ny, nz), F32)
         for j in range(per_vreg):
             c, x = divmod(g * per_vreg + j, nx)
-            acc = pack_z(acc, init[c, x], j)
-        sz[0, g] = acc
+            cell = init[c, x]
+            acc = pack_z(acc, cell, j)
+            acc2 = pack_z2(acc2, cell, j)
+        sz[0, g, 0] = acc
+        sz[0, g, 2] = acc2
+    pack_corners(0)
 
     pl.semaphore_wait(barrier, greeted)
     for g in range(2):
-        for i in (1, 2, 0):
-            start(functools.partial(face, 0, g), i)
+        send_exchange(0, g)
+    send_rest(0)
     loads[1].wait()
     for i in range(3):
         start(model_copy, i)
@@ -153,9 +286,9 @@
     for k in range(coup.shape[0]):
         kappa = jnp.where(classes == k, coup[k], kappa)
     scale = 0.8 / (36.0 + kappa * kappa)
-    ab[0] = 6.0 * scale
-    ab[1] = kappa * scale
-    ab[2] = kappa
+    const[chans] = 6.0 * scale
+    const[chans + 1] = kappa * scale
+    kap[...] = kappa
 
     def shifted(v):
         zero = jnp.zeros((1, ny, nz), F32)
@@ -167,7 +300,7 @@
         cells = init if s == 0 else f.at[s - 1]
 
         def one(p, carry):
-            a, b = ab[0], ab[1]
+            a, b = const[chans], const[chans + 1]
             fr, fi = cells[2 * p], cells[2 * p + 1]
             if s == 0:
                 sr, si = src[2 * p], src[2 * p + 1]
@@ -185,22 +318,25 @@
 
     ycor[...] = jnp.zeros(ycor.shape, F32)
 
+    def merge(low, high):
+        return jnp.where(even, low, pltpu.roll(high, nz - 2, 1))
+
     def finish(s, g):
         cells = out if s == SWEEPS - 1 else f.at[s]
         last = s == SWEEPS - 1
-        own_z = sz[s, g]
-        merged = jnp.where(
-            (lane & 1) == 0, hz[s, 0, g] - own_z, pltpu.roll(hz[s, 1, g] - own_z, nz - 2, 1)
-        )
+        deep = s % 2 == 1 and not last
+        own_z = sz[s, g, 0]
+        merged = merge(hz[s, 0, g, 0] - own_z, hz[s, 1, g, 0] - own_z)
         edge = (lane == 0) | (lane == nz - 1)
         rows = ycor.reshape(chans * nx * ny, nz)
-        for c in range(g * half, g * half + half):
+        for c in channels_of(g):
             for side, row in ((0, 0), (1, ny - 1)):
                 rows[pl.ds(c * nx * ny + row, nx, stride=ny), :] = (
                     hy[s, side, c] - sy[s, 1 - side, c]
                 )
 
-        def one(q, acc):
+        def one(q, accs):
+            acc, acc2 = accs
             c = g * half + 2 * q
             for x in range(nx):
                 sums = []
@@ -208,21 +344,116 @@
                     j = (2 * q + r) * nx + x
                     h = ycor[c + r, x] + jnp.where(edge, pltpu.roll(merged, nz - 2 * j, 1), 0.0)
                     if x == 0:
-                        h = h + hx[s, 0, c + r]
+                        h = h + hx[s, 0, c + r, 1]
                     if x == nx - 1:
-                        h = h + hx[s, 1, c + r]
+                        h = h + hx[s, 1, c + r, 0]
                     sums.append(h)
-                a, b = ab[0, x], ab[1, x]
+                a, b = const[chans, x], const[chans + 1, x]
                 nr = part_next[c, x] + (a * sums[0] + b * sums[1])
                 ni = part_next[c + 1, x] + (a * sums[1] - b * sums[0])
                 cells[c, x] = nr
                 cells[c + 1, x] = ni
-                if not last:
-                    acc = pack_z(acc, nr, 2 * q * nx + x)
-                    acc = pack_z(acc, ni, (2 * q + 1) * nx + x)
-            return acc
-
-        return lax.fori_loop(0, pairs // 2, one, jnp.zeros((ny, nz), F32), unroll=True)
+                for r, value in enumerate((nr, ni)):
+                    j = (2 * q + r) * nx + x
+                    if not last:
+                        acc = pack_z(acc, value, j)
+                    if deep:
+                        acc2 = pack_z2(acc2, value, j)
+            return acc, acc2
+
+        zero = jnp.zeros((ny, nz), F32)
+        acc, acc2 = lax.fori_loop(0, pairs // 2, one, (zero, zero), unroll=True)
+        if not last:
+            sz[s + 1, g, 0] = acc
+        if deep:
+            sz[s + 1, g, 2] = acc2
+
+    def stepped(fixed, field, total, a, b):
+        tr, ti = total
+        return (
+            fixed[0] + 0.2 * field[0] + (a * tr + b * ti),
+            fixed[1] + 0.2 * field[1] + (a * ti - b * tr),
+        )
+
+    def around(field, low, high, ends_z):
+        count = field.shape[0]
+        total = jnp.where(sub == 0, low, pltpu.roll(field, 1, 0))
+        total = total + jnp.where(sub == count - 1, high, pltpu.roll(field, count - 1, 0))
+        total = total + jnp.where(lane == 0, ends_z, pltpu.roll(field, 1, 1))
+        return total + jnp.where(lane == nz - 1, ends_z, pltpu.roll(field, nz - 1, 1))
+
+    def spread(row, count):
+        return jnp.broadcast_to(row, (count, nz))
+
+    def kept(i, side, value):
+        return jnp.where(has[i][side], value, 0.0)
+
+    def outer(e):
+        s = 2 * e
+        cells = init if e == 0 else f.at[s - 1]
+        both = [(g, side) for g in range(2) for side in range(2)]
+
+        for g, side in both:
+            v = hz[s, side, g, 0]
+            second = hz[s, side, g, 2]
+            if side == 1:
+                second = pltpu.roll(second, nz - 2, 1)
+            mine = pltpu.roll(sz[s, g, 0], nz - 1 if side == 0 else 1, 1)
+            low = spread(hyz[e, side, g, 0, ny - 1 : ny, :], ny)
+            high = spread(hyz[e, 2 + side, g, 0, 0:1, :], ny)
+            t = second + mine
+            t = t + jnp.where(sub == 0, low, pltpu.roll(v, 1, 0))
+            t = t + jnp.where(sub == ny - 1, high, pltpu.roll(v, ny - 1, 0))
+            over = 2 * (nx - 1)
+            t = t + jnp.where(
+                xlane == 0, pltpu.roll(hxz[e, side, g], nz - over, 1), pltpu.roll(v, 2, 1)
+            )
+            t = t + jnp.where(
+                xlane == nx - 1,
+                pltpu.roll(hxz[e, 2 + side, g], over, 1),
+                pltpu.roll(v, nz - 2, 1),
+            )
+            other = jnp.where(real, pltpu.roll(t, nz - 2 * nx, 1), -pltpu.roll(t, 2 * nx, 1))
+            new = hcz[side, g] + 0.2 * v + (hcz[side, 2] * t + hcz[side, 3] * other)
+            hz[s + 1, side, g, 0] = kept(2, side, new)
+
+        for g, side in both:
+            ends_z = merge(hyz[e, 2 * side, g, 1], hyz[e, 2 * side + 1, g, 1])
+            a, b = hcy[side, chans], hcy[side, chans + 1]
+            for q in range(half // 2):
+                c = g * half + 2 * q
+                fields, totals = [], []
+                for r in range(2):
+                    j = 2 * (2 * q + r) + 1 - side
+                    v = hy[s, side, c + r]
+                    low = spread(hxy[e, side, c + r : c + r + 1, :], nx)
+                    high = spread(hxy[e, 2 + side, c + r : c + r + 1, :], nx)
+                    t = around(v, low, high, pltpu.roll(ends_z, (nz - 2 * j) % nz, 1))
+                    fields.append(v)
+                    totals.append(t + hy2[e, side, c + r] + sy[s, side, c + r])
+                nr, ni = stepped((hcy[side, c], hcy[side, c + 1]), fields, totals, a, b)
+                hy[s + 1, side, c] = kept(1, side, nr)
+                hy[s + 1, side, c + 1] = kept(1, side, ni)
+
+        for g, side in both:
+            one, two = (1, 0) if side == 0 else (0, 1)
+            x = 0 if side == 0 else nx - 1
+            ends_z = merge(hxz[e, 2 * side, g], hxz[e, 2 * side + 1, g])
+            a, b = hcx[side, chans], hcx[side, chans + 1]
+            for q in range(half // 2):
+                c = g * half + 2 * q
+                fields, totals = [], []
+                for r in range(2):
+                    j = (2 * q + r) * nx + (nx - 1 - x)
+                    v = hx[s, side, c + r, one]
+                    low = spread(hxy[e, 2 * side, c + r : c + r + 1, :], ny)
+                    high = spread(hxy[e, 2 * side + 1, c + r : c + r + 1, :], ny)
+                    t = around(v, low, high, pltpu.roll(ends_z, (nz - 2 * j) % nz, 1))
+                    fields.append(v)
+                    totals.append(t + hx[s, side, c + r, two] + cells[c + r, x])
+                nr, ni = stepped((hcx[side, c], hcx[side, c + 1]), fields, totals, a, b)
+                hx[s + 1, side, c, one] = kept(0, side, nr)
+                hx[s + 1, side, c + 1, one] = kept(0, side, ni)
 
     groups = hi_hot.shape[0]
 
@@ -249,20 +480,47 @@
     loads[4].wait()
     for g in range(2):
         local(0, g)
-    hots(0, nx // SWEEPS)
-    for s in range(SWEEPS):
+    rows_of(const, scy, range(chans + 2), (0, ny - 1))
+    for g in range(4):
+        acc = jnp.zeros((ny, nz), F32)
+        for j in range(per_vreg if g < 2 else nx):
+            c, x = divmod(g * per_vreg + j, nx) if g < 2 else (chans + g - 2, j)
+            acc = pack_z(acc, const[c, x], j)
+        block = 2 * nx
+        while g >= 2 and block < nz:
+            acc = acc + pltpu.roll(acc, block, 1)
+            block *= 2
+        scz[g] = acc
+    for i in (1, 2, 0):
+        start(const_copy, i)
+    hots(0, nx // 2)
+    for e in range(SWEEPS // 2):
+        s = 2 * e
         for g in range(2):
             for i in (0, 2, 1):
-                wait_recv(functools.partial(face, s, g), i)
-            packed = finish(s, g)
-            if s < SWEEPS - 1:
-                sz[s + 1, g] = packed
-                pack_y(f.at[s], s + 1, g)
-                for i in (1, 2, 0):
-                    start(functools.partial(face, s + 1, g), i)
-                local(s + 1, g)
-        if s < SWEEPS - 1:
-            hots((s + 1) * nx // SWEEPS, (s + 2) * nx // SWEEPS)
+                wait_recv(functools.partial(face, e, g), i)
+            finish(s, g)
+            pack_rows(f.at[s], s + 1, g)
+            local(s + 1, g)
+        if e == 0:
+            for i in range(3):
+                wait_recv(const_copy, i)
+        wait_lines(e)
+        for g in range(2):
+            wait_recv(functools.partial(face, e, g), 3)
+        outer(e)
+        for g in range(2):
+            finish(s + 1, g)
+            if s + 2 < SWEEPS:
+                pack_exchange(f.at[s + 1], e + 1, g)
+                send_exchange(e + 1, g)
+        if s + 2 < SWEEPS:
+            pack_corners(e + 1)
+            send_rest(e + 1)
+            for g in range(2):
+                local(s + 2, g)
+            if e == 0:
+                hots(nx // 2, nx)
 
     def plane(x, total):
         sens = jnp.zeros((ny, nz), F32)
@@ -270,7 +528,7 @@
             fr, fi = out[2 * k, x], out[2 * k + 1, x]
             gr, gi = out[pairs + 2 * k, x], out[pairs + 2 * k + 1, x]
             sens = sens + (fr * gi + fi * gr)
-        sens = ab[2, x] * sens
+        sens = kap[x] * sens
         s0 = sens.astype(BF16).astype(F32)
         rest = sens - s0
         s1 = rest.astype(BF16).astype(F32)
@@ -318,6 +576,16 @@
     total = total + pltpu.roll(jnp.where(mlane == 0, hm[5], m), mz - 1, 2)
     smooth = 6.0 * m - total
 
+    for e in range(SWEEPS // 2):
+        for g in range(2):
+            for i in range(4):
+                wait_send(functools.partial(face, e, g), i)
+        wait_lines_sent(e)
+    for i in range(3):
+        wait_send(const_copy, i)
+    for i in range(3):
+        wait_send(model_copy, i)
+
     owned = part[pl.ds(pl.multiple_of(pos[2] * rows, rows), rows), :]
     for d in range(1, n):
         rs_copy(d).wait_recv()
@@ -327,12 +595,6 @@
     for k in range(m.shape[0]):
         grad[k] = owned[k * my : (k + 1) * my] + smooth[k]
 
-    for s in range(SWEEPS):
-        for g in range(2):
-            for i in range(3):
-                wait_send(functools.partial(face, s, g), i)
-    for i in range(3):
-        wait_send(model_copy, i)
     for d in range(1, n):
         rs_copy(d).wait_send()
 
@@ -375,22 +637,37 @@
                 pltpu.VMEM(model.shape, F32),
                 pltpu.VMEM((SWEEPS - 1, chans, nx, ny, nz), F32),
                 pltpu.VMEM((chans, nx, ny, nz), F32),
+                pltpu.VMEM((chans + 2, nx, ny, nz), F32),
+                pltpu.VMEM((nx, ny, nz), F32),
                 pltpu.VMEM((chans, nx, ny, nz), F32),
-                pltpu.VMEM((3, nx, ny, nz), F32),
-                pltpu.VMEM((chans, nx, ny, nz), F32),
-                pltpu.VMEM((SWEEPS, 2, chans, ny, nz), F32),
+                pltpu.VMEM((SWEEPS, 2, chans, 2, ny, nz), F32),
                 pltpu.VMEM((SWEEPS, 2, chans, nx, nz), F32),
-                pltpu.VMEM((SWEEPS, 2, 2, ny, nz), F32),
+                pltpu.VMEM((SWEEPS // 2, 2, chans, nx, nz), F32),
+                pltpu.VMEM((SWEEPS, 2, 2, 3, ny, nz), F32),
+                pltpu.VMEM((SWEEPS // 2, 4, 16, nz), F32),
+                pltpu.VMEM((SWEEPS // 2, 4, 2, ny, nz), F32),
+                pltpu.VMEM((SWEEPS // 2, 4, 2, 2, ny, nz), F32),
+                pltpu.VMEM((2, chans + 2, ny, nz), F32),
+                pltpu.VMEM((2, chans + 2, nx, nz), F32),
+                pltpu.VMEM((2, 4, ny, nz), F32),
                 pltpu.VMEM((SWEEPS, 2, chans, nx, nz), F32),
-                pltpu.VMEM((SWEEPS, 2, ny, nz), F32),
+                pltpu.VMEM((SWEEPS // 2, 2, chans, nx, nz), F32),
+                pltpu.VMEM((SWEEPS, 2, 3, ny, nz), F32),
+                pltpu.VMEM((SWEEPS // 2, 4, 16, nz), F32),
+                pltpu.VMEM((2, chans + 2, nx, nz), F32),
+                pltpu.VMEM((4, ny, nz), F32),
                 pltpu.VMEM((6,) + model.shape, F32),
                 pltpu.VMEM((nz, nx * ny * nz), BF16),
                 pltpu.VMEM((groups, nx * ny * nz), BF16),
                 pltpu.VMEM((groups, nz), F32),
                 pltpu.VMEM((n - 1, groups // n, nz), F32),
                 dma((6,)),
-                dma((SWEEPS, 2, 6)),
-                dma((SWEEPS, 2, 6)),
+                dma((SWEEPS // 2, 2, 8)),
+                dma((SWEEPS // 2, 2, 8)),
+                dma((SWEEPS // 2, 12)),
+                dma((SWEEPS // 2, 12)),
+                dma((6,)),
+                dma((6,)),
                 dma((6,)),
                 dma((6,)),
                 dma((n - 1,)),

time: 24.9 us -> 24.3 us (0.976)
  Pallas kernels: 24.2 us -> 23.5 us
    pallas_call x1, Pallas kernels: 23.4 us -> 22.7 us  [body(): pl.pallas_call(functools.partial(kernel, sizes), out_shape=(pltpu.VMEM(in...]
where the time goes in v3:
time: 24.3 us; the launch traced here: 24.1 us
  Pallas kernels  23.5 us (97%)
  between operations  0.64 us (3%)
    pallas_call x1, Pallas kernels, body(): pl.pallas_call(functools.partial(kernel, sizes), out_shape=(pltpu.VMEM(in...  22.7 us
    pallas_call x1, Pallas kernels, body(): pl.pallas_call(flush, out_shape=(jax.ShapeDtypeStruct(initial.shape, F32)...  0.77 us

profile of v3, /device:TPU:0, one launch (start us, length us, event | category | flops | bytes accessed | tf_op | source)
XLA Modules:
  0.0 24.1 jit_solution(7100424120655348970)
XLA Ops:
  0.6 22.7 %shard_map.77 = (f32[12,8,8,128]{3,2,1,0:T(8,128)S(1)}, f32[2,4,128]{2,1,0:T(4,128)S(1)}) custom-call(f32[12,8,8,128]{3,2,1,0:T(8,128)} %init_hbm.1, f32[12,8,8,128]{3,2,1,0:T(8,128)} %src_hbm.1, s32[8,8,128]{2,1,0:T(8,128)} %cls_hbm.1, f32[16]{0:T(128)} %coup_hbm.1, s32[8,8,128]{2,1,0:T(8,128)} %own_hbm.1, f32[2,4,128]{2,1,0:T(4,128)} %mod_hbm.1), custom_call_target="tpu_custom_call" | custom-call | tf_op jit(solution)/shard_map/pallas_call | solution.py:623
  23.3 0.8 %shard_map.78 = (f32[12,8,8,128]{3,2,1,0:T(8,128)}, f32[2,4,128]{2,1,0:T(4,128)}) custom-call(f32[12,8,8,128]{3,2,1,0:T(8,128)S(1)} %get-tuple-element.4.fields, f32[2,4,128]{2,1,0:T(4,128)S(1)} %get-tuple-element.5.grad), custom_call_target="tpu_custom_call" | custom-call | tf_op jit(solution)/shard_map/pallas_call | solution.py:680

commit v4 on v3

--- a/solution.py
+++ b/solution.py
@@ -17,7 +17,7 @@
 def kernel(
     sizes, init_hbm, src_hbm, cls_hbm, coup_hbm, own_hbm, mod_hbm, out, grad,
     init, src, cls, coup, own, mod, f, part_next, const, kap, ycor,
-    hx, hy, hy2, hz, hxy, hxz, hyz, hcx, hcy, hcz, sy, sy2, sz, sxy, scy, scz,
+    hx, hy, hz, hxy, hxz, hyz, hcx, hcy, hcz, sy, sz, sxy, syz, scy, scz,
     hm, lo_hot, hi_hot, part, rs,
     load_sem, send_sem, recv_sem, esend, erecv, csend, crecv, msend, mrecv, rsend, rrecv,
 ):
@@ -106,36 +106,33 @@
             line = held[m]
             line[:, 2 * si + sj] = jnp.zeros(line.shape[:1] + line.shape[2:], F32)
 
-    def face(e, g, i, side):
+    def face(e, i, side):
         s = 2 * e
         cells = init if e == 0 else f.at[s - 1]
-        mine = pl.ds(g * half, half)
-        axis = i
+        axis = min(i, 2)
         if i == 0:
-            source = cells.at[mine, pl.ds(0 if side == 0 else nx - 2, 2)]
-            halo = hx.at[s, 1 - side, mine]
-        elif i == 1:
-            source = sy.at[s, side, mine]
-            halo = hy.at[s, 1 - side, mine]
+            source = cells.at[:, pl.ds(0 if side == 0 else nx - 2, 2)]
+            halo = hx.at[s, 1 - side]
         elif i == 2:
-            source = sz.at[s, g]
-            halo = hz.at[s, 1 - side, g]
+            source = sz.at[s]
+            halo = hz.at[s, 1 - side]
         else:
             axis = 1
-            source = sy2.at[e, side, mine]
-            halo = hy2.at[e, 1 - side, mine]
+            mine = pl.ds(0 if i == 1 else half, half)
+            source = sy.at[s, side, :, mine]
+            halo = hy.at[s, 1 - side, :, mine]
         return pltpu.make_async_remote_copy(
             src_ref=source,
             dst_ref=halo,
-            send_sem=send_sem.at[e, g, 2 * i + side],
-            recv_sem=recv_sem.at[e, g, 2 * i + 1 - side],
+            send_sem=send_sem.at[e, 2 * i + side],
+            recv_sem=recv_sem.at[e, 2 * i + 1 - side],
             device_id={AXES[axis]: ends[axis][side]},
             device_id_type=MESH,
         )
 
     def line_copy(e, m, i, j, si, sj):
         s = 2 * e
-        source = (sxy.at[e, 2 * si + sj], sz.at[s, :, 0], sz.at[s, :, pl.ds(0, 2)])[m]
+        source = (sxy.at[e, 2 * si + sj], sz.at[s, :, 0], syz.at[e])[m]
         there = 2 * (1 - si) + 1 - sj
         return pltpu.make_async_remote_copy(
             src_ref=source,
@@ -214,12 +211,6 @@
             def _():
                 make(i, side).wait_send()
 
-    def rows_of(cells, into, channels, rows):
-        flat = cells.reshape(cells.shape[0] * nx * ny, nz)
-        for c in channels:
-            for side, row in enumerate(rows):
-                into[side, c] = flat[pl.ds(c * nx * ny + row, nx, stride=ny), :]
-
     def channels_of(g):
         return range(g * half, g * half + half)
 
@@ -229,37 +220,32 @@
     def pack_z2(acc, value, j):
         return jnp.where(shift3 == 2 * j, pltpu.roll(value, 2 * j + 2, 1), acc)
 
-    def pack_rows(cells, s, g):
-        rows_of(cells, sy.at[s], channels_of(g), (0, ny - 1))
-
-    def pack_exchange(cells, e, g):
+    def pack_rows(cells, s, g, layer=0):
+        flat = cells.reshape(chans * nx * ny, nz)
+        for c in channels_of(g):
+            for side, row in enumerate((layer, ny - 1 - layer)):
+                sy[s, side, layer, c] = flat[pl.ds(c * nx * ny + row, nx, stride=ny), :]
+
+    def pack_lines(e):
         s = 2 * e
-        pack_rows(cells, s, g)
-        rows_of(cells, sy2.at[e], channels_of(g), (1, ny - 2))
         acc = jnp.zeros((nx, nz), F32)
-        for k in range(half):
+        for c in range(chans):
             for side in range(2):
-                acc = pack_z(acc, sy[s, side, g * half + k], 2 * k + side)
-        sz[s, g, 1] = acc
-
-    def pack_corners(e):
+                acc = pack_z(acc, sy[s, side, 0, c], 2 * c + side)
+        syz[e, 0] = acc
+        for g in range(2):
+            for side, row in enumerate((0, ny - 1)):
+                at = 2 * side + g
+                syz[e, 1, at : at + 1, :] = sz[s, g, 0, row : row + 1, :]
         for side in range(2):
-            flat = sy.at[2 * e, side].reshape(chans * nx, nz)
+            flat = sy.at[s, side, 0].reshape(chans * nx, nz)
             for end, x in enumerate((0, nx - 1)):
                 sxy[e, 2 * end + side, 0:chans] = flat[pl.ds(x, chans, stride=nx), :]
 
-    def send_exchange(e, g):
-        for i in (1, 2, 0):
-            start(functools.partial(face, e, g), i)
-
-    def send_rest(e):
-        for g in range(2):
-            start(functools.partial(face, e, g), 3)
-        start_lines(e)
-
     loads[0].wait()
     for g in range(2):
-        pack_exchange(init, 0, g)
+        pack_rows(init, 0, g)
+        pack_rows(init, 0, g, 1)
         acc = jnp.zeros((ny, nz), F32)
         acc2 = jnp.zeros((ny, nz), F32)
         for j in range(per_vreg):
@@ -268,13 +254,13 @@
             acc = pack_z(acc, cell, j)
             acc2 = pack_z2(acc2, cell, j)
         sz[0, g, 0] = acc
-        sz[0, g, 2] = acc2
-    pack_corners(0)
+        sz[0, g, 1] = acc2
+    pack_lines(0)
 
     pl.semaphore_wait(barrier, greeted)
-    for g in range(2):
-        send_exchange(0, g)
-    send_rest(0)
+    for i in (1, 3, 2, 0):
+        start(functools.partial(face, 0), i)
+    start_lines(0)
     loads[1].wait()
     for i in range(3):
         start(model_copy, i)
@@ -332,7 +318,7 @@
         for c in channels_of(g):
             for side, row in ((0, 0), (1, ny - 1)):
                 rows[pl.ds(c * nx * ny + row, nx, stride=ny), :] = (
-                    hy[s, side, c] - sy[s, 1 - side, c]
+                    hy[s, side, 0, c] - sy[s, 1 - side, 0, c]
                 )
 
         def one(q, accs):
@@ -366,7 +352,7 @@
         if not last:
             sz[s + 1, g, 0] = acc
         if deep:
-            sz[s + 1, g, 2] = acc2
+            sz[s + 1, g, 1] = acc2
 
     def stepped(fixed, field, total, a, b):
         tr, ti = total
@@ -388,19 +374,19 @@
     def kept(i, side, value):
         return jnp.where(has[i][side], value, 0.0)
 
-    def outer(e):
+    def outer(e, only):
         s = 2 * e
         cells = init if e == 0 else f.at[s - 1]
-        both = [(g, side) for g in range(2) for side in range(2)]
+        both = [(g, side) for g in only for side in range(2)]
 
         for g, side in both:
             v = hz[s, side, g, 0]
-            second = hz[s, side, g, 2]
+            second = hz[s, side, g, 1]
             if side == 1:
                 second = pltpu.roll(second, nz - 2, 1)
             mine = pltpu.roll(sz[s, g, 0], nz - 1 if side == 0 else 1, 1)
-            low = spread(hyz[e, side, g, 0, ny - 1 : ny, :], ny)
-            high = spread(hyz[e, 2 + side, g, 0, 0:1, :], ny)
+            low = spread(hyz[e, side, 1, 2 + g : 3 + g, :], ny)
+            high = spread(hyz[e, 2 + side, 1, g : g + 1, :], ny)
             t = second + mine
             t = t + jnp.where(sub == 0, low, pltpu.roll(v, 1, 0))
             t = t + jnp.where(sub == ny - 1, high, pltpu.roll(v, ny - 1, 0))
@@ -418,22 +404,22 @@
             hz[s + 1, side, g, 0] = kept(2, side, new)
 
         for g, side in both:
-            ends_z = merge(hyz[e, 2 * side, g, 1], hyz[e, 2 * side + 1, g, 1])
+            ends_z = merge(hyz[e, 2 * side, 0], hyz[e, 2 * side + 1, 0])
             a, b = hcy[side, chans], hcy[side, chans + 1]
             for q in range(half // 2):
                 c = g * half + 2 * q
                 fields, totals = [], []
                 for r in range(2):
-                    j = 2 * (2 * q + r) + 1 - side
-                    v = hy[s, side, c + r]
+                    j = 2 * (c + r) + 1 - side
+                    v = hy[s, side, 0, c + r]
                     low = spread(hxy[e, side, c + r : c + r + 1, :], nx)
                     high = spread(hxy[e, 2 + side, c + r : c + r + 1, :], nx)
                     t = around(v, low, high, pltpu.roll(ends_z, (nz - 2 * j) % nz, 1))
                     fields.append(v)
-                    totals.append(t + hy2[e, side, c + r] + sy[s, side, c + r])
+                    totals.append(t + hy[s, side, 1, c + r] + sy[s, side, 0, c + r])
                 nr, ni = stepped((hcy[side, c], hcy[side, c + 1]), fields, totals, a, b)
-                hy[s + 1, side, c] = kept(1, side, nr)
-                hy[s + 1, side, c + 1] = kept(1, side, ni)
+                hy[s + 1, side, 0, c] = kept(1, side, nr)
+                hy[s + 1, side, 0, c + 1] = kept(1, side, ni)
 
         for g, side in both:
             one, two = (1, 0) if side == 0 else (0, 1)
@@ -480,7 +466,10 @@
     loads[4].wait()
     for g in range(2):
         local(0, g)
-    rows_of(const, scy, range(chans + 2), (0, ny - 1))
+    flat = const.reshape((chans + 2) * nx * ny, nz)
+    for c in range(chans + 2):
+        for side, row in enumerate((0, ny - 1)):
+            scy[side, c] = flat[pl.ds(c * nx * ny + row, nx, stride=ny), :]
     for g in range(4):
         acc = jnp.zeros((ny, nz), F32)
         for j in range(per_vreg if g < 2 else nx):
@@ -497,8 +486,8 @@
     for e in range(SWEEPS // 2):
         s = 2 * e
         for g in range(2):
-            for i in (0, 2, 1):
-                wait_recv(functools.partial(face, e, g), i)
+            for i in (1, 0, 2) if g == 0 else (3,):
+                wait_recv(functools.partial(face, e), i)
             finish(s, g)
             pack_rows(f.at[s], s + 1, g)
             local(s + 1, g)
@@ -507,16 +496,17 @@
                 wait_recv(const_copy, i)
         wait_lines(e)
         for g in range(2):
-            wait_recv(functools.partial(face, e, g), 3)
-        outer(e)
-        for g in range(2):
+            outer(e, (g,))
             finish(s + 1, g)
             if s + 2 < SWEEPS:
-                pack_exchange(f.at[s + 1], e + 1, g)
-                send_exchange(e + 1, g)
+                pack_rows(f.at[s + 1], s + 2, g)
+                pack_rows(f.at[s + 1], s + 2, g, 1)
+                start(functools.partial(face, e + 1), 1 + 2 * g)
         if s + 2 < SWEEPS:
-            pack_corners(e + 1)
-            send_rest(e + 1)
+            for i in (2, 0):
+                start(functools.partial(face, e + 1), i)
+            pack_lines(e + 1)
+            start_lines(e + 1)
             for g in range(2):
                 local(s + 2, g)
             if e == 0:
@@ -577,9 +567,8 @@
     smooth = 6.0 * m - total
 
     for e in range(SWEEPS // 2):
-        for g in range(2):
-            for i in range(4):
-                wait_send(functools.partial(face, e, g), i)
+        for i in range(4):
+            wait_send(functools.partial(face, e), i)
         wait_lines_sent(e)
     for i in range(3):
         wait_send(const_copy, i)
@@ -641,19 +630,18 @@
                 pltpu.VMEM((nx, ny, nz), F32),
                 pltpu.VMEM((chans, nx, ny, nz), F32),
                 pltpu.VMEM((SWEEPS, 2, chans, 2, ny, nz), F32),
-                pltpu.VMEM((SWEEPS, 2, chans, nx, nz), F32),
-                pltpu.VMEM((SWEEPS // 2, 2, chans, nx, nz), F32),
-                pltpu.VMEM((SWEEPS, 2, 2, 3, ny, nz), F32),
+                pltpu.VMEM((SWEEPS, 2, 2, chans, nx, nz), F32),
+                pltpu.VMEM((SWEEPS, 2, 2, 2, ny, nz), F32),
                 pltpu.VMEM((SWEEPS // 2, 4, 16, nz), F32),
                 pltpu.VMEM((SWEEPS // 2, 4, 2, ny, nz), F32),
-                pltpu.VMEM((SWEEPS // 2, 4, 2, 2, ny, nz), F32),
+                pltpu.VMEM((SWEEPS // 2, 4, 2, ny, nz), F32),
                 pltpu.VMEM((2, chans + 2, ny, nz), F32),
                 pltpu.VMEM((2, chans + 2, nx, nz), F32),
                 pltpu.VMEM((2, 4, ny, nz), F32),
-                pltpu.VMEM((SWEEPS, 2, chans, nx, nz), F32),
-                pltpu.VMEM((SWEEPS // 2, 2, chans, nx, nz), F32),
-                pltpu.VMEM((SWEEPS, 2, 3, ny, nz), F32),
+                pltpu.VMEM((SWEEPS, 2, 2, chans, nx, nz), F32),
+                pltpu.VMEM((SWEEPS, 2, 2, ny, nz), F32),
                 pltpu.VMEM((SWEEPS // 2, 4, 16, nz), F32),
+                pltpu.VMEM((SWEEPS // 2, 2, ny, nz), F32),
                 pltpu.VMEM((2, chans + 2, nx, nz), F32),
                 pltpu.VMEM((4, ny, nz), F32),
                 pltpu.VMEM((6,) + model.shape, F32),
@@ -662,8 +650,8 @@
                 pltpu.VMEM((groups, nz), F32),
                 pltpu.VMEM((n - 1, groups // n, nz), F32),
                 dma((6,)),
-                dma((SWEEPS // 2, 2, 8)),
-                dma((SWEEPS // 2, 2, 8)),
+                dma((SWEEPS // 2, 8)),
+                dma((SWEEPS // 2, 8)),
                 dma((SWEEPS // 2, 12)),
                 dma((SWEEPS // 2, 12)),
                 dma((6,)),

time: 24.3 us -> 23.3 us (0.959)
  Pallas kernels: 23.5 us -> 22.5 us
    pallas_call x1, Pallas kernels: 22.7 us -> 21.8 us  [body(): pl.pallas_call(functools.partial(kernel, sizes), out_shape=(pltpu.VMEM(in...]
where the time goes in v4:
time: 23.3 us; the launch traced here: 23.2 us
  Pallas kernels  22.5 us (97%)
  between operations  0.64 us (3%)
    pallas_call x1, Pallas kernels, body(): pl.pallas_call(functools.partial(kernel, sizes), out_shape=(pltpu.VMEM(in...  21.8 us
    pallas_call x1, Pallas kernels, body(): pl.pallas_call(flush, out_shape=(jax.ShapeDtypeStruct(initial.shape, F32)...  0.77 us

profile of v4, /device:TPU:0, one launch (start us, length us, event | category | flops | bytes accessed | tf_op | source)
XLA Modules:
  0.0 23.2 jit_solution(17767118241353678408)
XLA Ops:
  0.6 21.8 %shard_map.77 = (f32[12,8,8,128]{3,2,1,0:T(8,128)S(1)}, f32[2,4,128]{2,1,0:T(4,128)S(1)}) custom-call(f32[12,8,8,128]{3,2,1,0:T(8,128)} %init_hbm.1, f32[12,8,8,128]{3,2,1,0:T(8,128)} %src_hbm.1, s32[8,8,128]{2,1,0:T(8,128)} %cls_hbm.1, f32[16]{0:T(128)} %coup_hbm.1, s32[8,8,128]{2,1,0:T(8,128)} %own_hbm.1, f32[2,4,128]{2,1,0:T(4,128)} %mod_hbm.1), custom_call_target="tpu_custom_call" | custom-call | tf_op jit(solution)/shard_map/pallas_call | solution.py:612
  22.4 0.8 %shard_map.78 = (f32[12,8,8,128]{3,2,1,0:T(8,128)}, f32[2,4,128]{2,1,0:T(4,128)}) custom-call(f32[12,8,8,128]{3,2,1,0:T(8,128)S(1)} %get-tuple-element.4.fields, f32[2,4,128]{2,1,0:T(4,128)S(1)} %get-tuple-element.5.grad), custom_call_target="tpu_custom_call" | custom-call | tf_op jit(solution)/shard_map/pallas_call | solution.py:668

commit v5 on v4

--- a/solution.py
+++ b/solution.py
@@ -37,40 +37,6 @@
         for sj in range(2)
     ]
 
-    barrier = pltpu.get_barrier_semaphore()
-    for i in range(2):
-        for side in range(2):
-
-            @pl.when(has[i][side])
-            def _():
-                pl.semaphore_signal(
-                    barrier, inc=1, device_id={AXES[i]: ends[i][side]}, device_id_type=MESH
-                )
-
-    for d in range(1, n):
-        pl.semaphore_signal(barrier, inc=1, device_id={"gz": peers[d - 1]}, device_id_type=MESH)
-
-    def met(i, j, si, sj):
-        return jnp.logical_and(has[i][si], has[j][sj])
-
-    for m, i, j, si, sj in lines:
-
-        @pl.when(met(i, j, si, sj))
-        def _():
-            pl.semaphore_signal(
-                barrier,
-                inc=1,
-                device_id={AXES[i]: ends[i][si], AXES[j]: ends[j][sj]},
-                device_id_type=MESH,
-            )
-
-    greeted = n - 1
-    for i in range(2):
-        for side in range(2):
-            greeted = greeted + has[i][side].astype(jnp.int32)
-    for m, i, j, si, sj in lines:
-        greeted = greeted + met(i, j, si, sj).astype(jnp.int32)
-
     loads = [
         pltpu.make_async_copy(a, b, load_sem.at[k])
         for k, (a, b) in enumerate(
@@ -80,7 +46,42 @@
             )
         )
     ]
-    for load in loads:
+    loads[0].start()
+    barrier = pltpu.get_barrier_semaphore()
+    for i in range(2):
+        for side in range(2):
+
+            @pl.when(has[i][side])
+            def _():
+                pl.semaphore_signal(
+                    barrier, inc=1, device_id={AXES[i]: ends[i][side]}, device_id_type=MESH
+                )
+
+    for d in range(1, n):
+        pl.semaphore_signal(barrier, inc=1, device_id={"gz": peers[d - 1]}, device_id_type=MESH)
+
+    def met(i, j, si, sj):
+        return jnp.logical_and(has[i][si], has[j][sj])
+
+    for m, i, j, si, sj in lines:
+
+        @pl.when(met(i, j, si, sj))
+        def _():
+            pl.semaphore_signal(
+                barrier,
+                inc=1,
+                device_id={AXES[i]: ends[i][si], AXES[j]: ends[j][sj]},
+                device_id_type=MESH,
+            )
+
+    greeted = n - 1
+    for i in range(2):
+        for side in range(2):
+            greeted = greeted + has[i][side].astype(jnp.int32)
+    for m, i, j, si, sj in lines:
+        greeted = greeted + met(i, j, si, sj).astype(jnp.int32)
+
+    for load in loads[1:]:
         load.start()
 
     lane = lax.broadcasted_iota(jnp.int32, (ny, nz), 1)
@@ -167,16 +168,18 @@
     def const_copy(i, side):
         if i == 0:
             source, halo = const.at[:, 0 if side == 0 else nx - 1], hcx
-        elif i == 1:
-            source, halo = scy.at[side], hcy
+            halo = halo.at[1 - side]
+        elif i == 2:
+            source, halo = scz, hcz.at[1 - side]
         else:
-            source, halo = scz, hcz
+            some = pl.ds(0, half + 2) if i == 1 else pl.ds(half + 2, half)
+            source, halo = scy.at[side, some], hcy.at[1 - side, some]
         return pltpu.make_async_remote_copy(
             src_ref=source,
-            dst_ref=halo.at[1 - side],
+            dst_ref=halo,
             send_sem=csend.at[2 * i + side],
             recv_sem=crecv.at[2 * i + 1 - side],
-            device_id={AXES[i]: ends[i][side]},
+            device_id={AXES[i % 2 if i == 3 else i]: ends[i % 2 if i == 3 else i][side]},
             device_id_type=MESH,
         )
 
@@ -258,15 +261,13 @@
     pack_lines(0)
 
     pl.semaphore_wait(barrier, greeted)
-    for i in (1, 3, 2, 0):
+    for i in (1, 2, 0):
         start(functools.partial(face, 0), i)
     start_lines(0)
-    loads[1].wait()
-    for i in range(3):
-        start(model_copy, i)
 
     loads[2].wait()
     loads[5].wait()
+    loads[3].wait()
     classes = cls[...]
     kappa = jnp.zeros(classes.shape, F32)
     for k in range(coup.shape[0]):
@@ -288,13 +289,7 @@
         def one(p, carry):
             a, b = const[chans], const[chans + 1]
             fr, fi = cells[2 * p], cells[2 * p + 1]
-            if s == 0:
-                sr, si = src[2 * p], src[2 * p + 1]
-                cr, ci = a * sr + b * si, a * si - b * sr
-                const[2 * p] = cr
-                const[2 * p + 1] = ci
-            else:
-                cr, ci = const[2 * p], const[2 * p + 1]
+            cr, ci = const[2 * p], const[2 * p + 1]
             tr, ti = shifted(fr), shifted(fi)
             part_next[2 * p] = cr + 0.2 * fr + (a * tr + b * ti)
             part_next[2 * p + 1] = ci + 0.2 * fi + (a * ti - b * tr)
@@ -405,7 +400,7 @@
 
         for g, side in both:
             ends_z = merge(hyz[e, 2 * side, 0], hyz[e, 2 * side + 1, 0])
-            a, b = hcy[side, chans], hcy[side, chans + 1]
+            a, b = hcy[side, 0], hcy[side, 1]
             for q in range(half // 2):
                 c = g * half + 2 * q
                 fields, totals = [], []
@@ -417,7 +412,7 @@
                     t = around(v, low, high, pltpu.roll(ends_z, (nz - 2 * j) % nz, 1))
                     fields.append(v)
                     totals.append(t + hy[s, side, 1, c + r] + sy[s, side, 0, c + r])
-                nr, ni = stepped((hcy[side, c], hcy[side, c + 1]), fields, totals, a, b)
+                nr, ni = stepped((hcy[side, c + 2], hcy[side, c + 3]), fields, totals, a, b)
                 hy[s + 1, side, 0, c] = kept(1, side, nr)
                 hy[s + 1, side, 0, c + 1] = kept(1, side, ni)
 
@@ -462,14 +457,29 @@
 
         lax.fori_loop(x0, x1, one, 0, unroll=True)
 
-    loads[3].wait()
     loads[4].wait()
+    flat = const.reshape((chans + 2) * nx * ny, nz)
+
+    def pack_const(into, c):
+        for side, row in enumerate((0, ny - 1)):
+            scy[side, into] = flat[pl.ds(c * nx * ny + row, nx, stride=ny), :]
+
+    a, b = const[chans], const[chans + 1]
+    for r in range(2):
+        pack_const(r, chans + r)
     for g in range(2):
-        local(0, g)
-    flat = const.reshape((chans + 2) * nx * ny, nz)
-    for c in range(chans + 2):
-        for side, row in enumerate((0, ny - 1)):
-            scy[side, c] = flat[pl.ds(c * nx * ny + row, nx, stride=ny), :]
+        for c in range(g * half, g * half + half, 2):
+            sr, si = src[c], src[c + 1]
+            const[c] = a * sr + b * si
+            const[c + 1] = a * si - b * sr
+            pack_const(c + 2, c)
+            pack_const(c + 3, c + 1)
+        if g == 0:
+            start(const_copy, 1)
+            start(functools.partial(face, 0), 3)
+        else:
+            start(const_copy, 3)
+            start(const_copy, 0)
     for g in range(4):
         acc = jnp.zeros((ny, nz), F32)
         for j in range(per_vreg if g < 2 else nx):
@@ -480,28 +490,46 @@
             acc = acc + pltpu.roll(acc, block, 1)
             block *= 2
         scz[g] = acc
-    for i in (1, 2, 0):
-        start(const_copy, i)
+    start(const_copy, 2)
+    loads[1].wait()
+    for i in range(3):
+        start(model_copy, i)
+    for g in range(2):
+        local(0, g)
     hots(0, nx // 2)
+    def first(e, g):
+        s = 2 * e
+        for i in (1, 0, 2) if g == 0 else (3,):
+            wait_recv(functools.partial(face, e), i)
+        finish(s, g)
+        pack_rows(f.at[s], s + 1, g)
+        local(s + 1, g)
+
+    def second(e, g):
+        s = 2 * e
+        if e == 0:
+            for i in (0, 2, 1) if g == 0 else (3,):
+                wait_recv(const_copy, i)
+        if g == 0:
+            wait_lines(e)
+        outer(e, (g,))
+        finish(s + 1, g)
+        if s + 2 < SWEEPS:
+            pack_rows(f.at[s + 1], s + 2, g)
+            pack_rows(f.at[s + 1], s + 2, g, 1)
+            start(functools.partial(face, e + 1), 1 + 2 * g)
+
     for e in range(SWEEPS // 2):
         s = 2 * e
-        for g in range(2):
-            for i in (1, 0, 2) if g == 0 else (3,):
-                wait_recv(functools.partial(face, e), i)
-            finish(s, g)
-            pack_rows(f.at[s], s + 1, g)
-            local(s + 1, g)
         if e == 0:
-            for i in range(3):
-                wait_recv(const_copy, i)
-        wait_lines(e)
-        for g in range(2):
-            outer(e, (g,))
-            finish(s + 1, g)
-            if s + 2 < SWEEPS:
-                pack_rows(f.at[s + 1], s + 2, g)
-                pack_rows(f.at[s + 1], s + 2, g, 1)
-                start(functools.partial(face, e + 1), 1 + 2 * g)
+            for g in range(2):
+                first(e, g)
+                second(e, g)
+        else:
+            for g in range(2):
+                first(e, g)
+            for g in range(2):
+                second(e, g)
         if s + 2 < SWEEPS:
             for i in (2, 0):
                 start(functools.partial(face, e + 1), i)
@@ -570,7 +598,7 @@
         for i in range(4):
             wait_send(functools.partial(face, e), i)
         wait_lines_sent(e)
-    for i in range(3):
+    for i in range(4):
         wait_send(const_copy, i)
     for i in range(3):
         wait_send(model_copy, i)
@@ -654,8 +682,8 @@
                 dma((SWEEPS // 2, 8)),
                 dma((SWEEPS // 2, 12)),
                 dma((SWEEPS // 2, 12)),
-                dma((6,)),
-                dma((6,)),
+                dma((8,)),
+                dma((8,)),
                 dma((6,)),
                 dma((6,)),
                 dma((n - 1,)),

time: 23.3 us -> 22.7 us (0.974)
  Pallas kernels: 22.5 us -> 21.9 us
    pallas_call x1, Pallas kernels: 21.8 us -> 21.1 us  [body(): pl.pallas_call(functools.partial(kernel, sizes), out_shape=(pltpu.VMEM(in...]
where the time goes in v5:
time: 22.7 us; the launch traced here: 22.5 us
  Pallas kernels  21.9 us (96%)
  between operations  0.64 us (3%)
    pallas_call x1, Pallas kernels, body(): pl.pallas_call(functools.partial(kernel, sizes), out_shape=(pltpu.VMEM(in...  21.1 us
    pallas_call x1, Pallas kernels, body(): pl.pallas_call(flush, out_shape=(jax.ShapeDtypeStruct(initial.shape, F32)...  0.77 us

profile of v5, /device:TPU:0, one launch (start us, length us, event | category | flops | bytes accessed | tf_op | source)
XLA Modules:
  0.0 22.5 jit_solution(12702648191330941096)
XLA Ops:
  0.6 21.1 %shard_map.77 = (f32[12,8,8,128]{3,2,1,0:T(8,128)S(1)}, f32[2,4,128]{2,1,0:T(4,128)S(1)}) custom-call(f32[12,8,8,128]{3,2,1,0:T(8,128)} %init_hbm.1, f32[12,8,8,128]{3,2,1,0:T(8,128)} %src_hbm.1, s32[8,8,128]{2,1,0:T(8,128)} %cls_hbm.1, f32[16]{0:T(128)} %coup_hbm.1, s32[8,8,128]{2,1,0:T(8,128)} %own_hbm.1, f32[2,4,128]{2,1,0:T(4,128)} %mod_hbm.1), custom_call_target="tpu_custom_call" | custom-call | tf_op jit(solution)/shard_map/pallas_call | solution.py:640
  21.7 0.8 %shard_map.78 = (f32[12,8,8,128]{3,2,1,0:T(8,128)}, f32[2,4,128]{2,1,0:T(4,128)}) custom-call(f32[12,8,8,128]{3,2,1,0:T(8,128)S(1)} %get-tuple-element.4.fields, f32[2,4,128]{2,1,0:T(4,128)S(1)} %get-tuple-element.5.grad), custom_call_target="tpu_custom_call" | custom-call | tf_op jit(solution)/shard_map/pallas_call | solution.py:696
